TPU v7x, 128 devices: a whole 4x4x4 slice. The times are simulated.
128 devices in a mesh: group: 8 (over z, core), rank: 16 (over x, y).
Axes of the slice: x: 4, y: 4, z: 4, core: 2. Of those that a mesh axis runs over, the one named last changes fastest.
Arguments:
- grad_out: bfloat16 [65536, 768], P(('group', 'rank')), may hold values from -6 to 6
- gate_prob: float32 [65536], P(('group', 'rank')), may hold values from 0.2 to 1
- expert_index: int32 [65536], P(('group', 'rank')), may hold values from 0 to 127
- slot: int32 [65536], P(('group', 'rank')), may hold values from -1 to 7, as said below
- saved_inputs: bfloat16 [128, 1024, 768], P(('group', 'rank')), may hold values from -6 to 6
- w_in: bfloat16 [128, 768, 2048], P(('group', 'rank')), may hold values from -0.21875 to 0.21875
- w_out: bfloat16 [128, 2048, 768], P(('group', 'rank')), may hold values from -0.125 to 0.125
Outputs:
- grad_in: bfloat16 [65536, 768], P(('group', 'rank'))
- grad_w_in: float32 [128, 768, 2048], P(('group', 'rank'))
- grad_w_out: float32 [128, 2048, 768], P(('group', 'rank'))
Inputs may be any that keep to these rules, and one draw needn't show every extreme that they name: slot[t] is the number of earlier tokens of the same device with the same expert, or -1 where that number is 8 or more.
All inputs are finite; a program needn't handle non-finite values.
Results may differ from a plain program's by a relative error of at most 0.018.
Values may be sent and summed in bfloat16 or wider, within the bound.
A program may use at most 128 MiB of HBM per device.

v0:
```python
import jax
import jax.numpy as jnp
from jax import lax
from jax.sharding import PartitionSpec as P


def local(grad_out, gate_prob, expert_index, slot, saved_inputs, w_in, w_out):
    groups = lax.axis_size("group")
    ranks = lax.axis_size("rank")
    experts = groups * ranks
    tok_rows = grad_out.shape[0]
    width = grad_out.shape[1]
    capacity = saved_inputs.shape[1] // experts
    scaled = (gate_prob[:, None] * grad_out.astype(jnp.float32)).astype(jnp.bfloat16)
    kept = slot >= 0
    target = jnp.where(kept, expert_index * capacity + slot, -1)
    table = (
        lax.broadcasted_iota(jnp.int32, (experts * capacity, tok_rows), 0) == target[None, :]
    ).astype(jnp.bfloat16)
    outgoing = jnp.dot(table, scaled, preferred_element_type=jnp.float32).astype(jnp.bfloat16)
    arrived = lax.all_to_all(
        outgoing.reshape(experts, capacity, width),
        ("group", "rank"),
        split_axis=0,
        concat_axis=1,
        tiled=True,
    )
    grad_rows = arrived.reshape(experts * capacity, width)
    inputs = saved_inputs[0]
    first = w_in[0]
    second = w_out[0]
    pre = jnp.dot(inputs, first, preferred_element_type=jnp.float32)
    hidden = jnp.maximum(pre, 0.0).astype(jnp.bfloat16)
    grad_second = lax.dot_general(
        hidden, grad_rows, (((0,), (0,)), ((), ())), preferred_element_type=jnp.float32
    )
    back_hidden = lax.dot_general(
        grad_rows, second, (((1,), (1,)), ((), ())), preferred_element_type=jnp.float32
    )
    grad_hidden = jnp.where(pre > 0, back_hidden, jnp.zeros_like(back_hidden)).astype(jnp.bfloat16)
    grad_first = lax.dot_general(
        inputs, grad_hidden, (((0,), (0,)), ((), ())), preferred_element_type=jnp.float32
    )
    row_grad = lax.dot_general(
        grad_hidden, first, (((1,), (1,)), ((), ())), preferred_element_type=jnp.float32
    ).astype(jnp.bfloat16)
    returned = lax.all_to_all(
        row_grad.reshape(1, experts * capacity, width),
        ("group", "rank"),
        split_axis=1,
        concat_axis=0,
        tiled=True,
    )
    flat_back = returned.reshape(experts * capacity, width)
    taken = jnp.take(flat_back, jnp.maximum(target, 0), axis=0)
    grad_in = jnp.where(kept[:, None], taken, jnp.zeros_like(taken))
    return (grad_in, grad_first[None], grad_second[None])


def solution(mesh):
    in_specs = (
        P(("group", "rank"), None),
        P(("group", "rank")),
        P(("group", "rank")),
        P(("group", "rank")),
        P(("group", "rank"), None, None),
        P(("group", "rank"), None, None),
        P(("group", "rank"), None, None),
    )
    out_specs = (
        P(("group", "rank"), None),
        P(("group", "rank"), None, None),
        P(("group", "rank"), None, None),
    )
    return jax.shard_map(local, mesh=mesh, in_specs=in_specs, out_specs=out_specs, check_vma=False)
```

profile of v0, /device:TPU:1, one launch (start us, length us, event | category | flops | bytes accessed | tf_op | source)
XLA Modules:
  0.0 126.2 jit_solution(14209305888620083234)
XLA Ops:
  0.6 0.0 copy-start
  0.6 0.9 broadcast_compare_fusion
  1.5 3.5 %fusion.20 = bf16[128,8,768]{2,1,0:T(8,128)(2,1)} fusion(s32[512]{0:T(512)S(1)} %get-tuple-element.13, bf16[512,768]{1,0:T(8,128)(2,1)} %param.7, f32[512]{0:T(512)} %param.8), kind=kOutput, calls=%fused_computation.23 | convolution fusion | flops 807796736 | bytes 2363392 | tf_op jit(solution)/shard_map/dot_general | solution.py:20
  5.0 11.9 %all-to-all-start = ((bf16[128,8,768]{2,1,0:T(8,128)(2,1)}), bf16[128,8,768]{2,1,0:T(8,128)(2,1)}, u32[]{:S(2)}, u32[]{:S(2)}) async-start(bf16[128,8,768]{2,1,0:T(8,128)(2,1)} %fusion.20), calls=%async_computation | async-start | bytes 3145728 | tf_op jit(solution)/shard_map/all_to_all | solution.py:21
  17.0 0.0 copy-done
  17.0 7.1 %fusion.6 = f32[1024,2048]{1,0:T(8,128)} fusion(bf16[1,768,2048]{2,1,0:T(8,128)(2,1)S(1)} %copy-done, bf16[1,1024,768]{2,1,0:T(8,128)(2,1)} %param.11), kind=kOutput, calls=%fused_computation.10 | convolution fusion | flops 3221225472 | bytes 13107200 | tf_op jit(solution)/shard_map/dot_general | solution.py:32
  24.1 16.7 %all-to-all-done = bf16[128,8,768]{2,1,0:T(8,128)(2,1)} async-done(((bf16[128,8,768]{2,1,0:T(8,128)(2,1)}), bf16[128,8,768]{2,1,0:T(8,128)(2,1)}, u32[]{:S(2)}, u32[]{:S(2)}) %all-to-all-start) | async-done | bytes 1572896 | tf_op jit(solution)/shard_map/all_to_all | solution.py:21
  40.8 8.3 %select_convert_fusion = bf16[1024,2048]{1,0:T(8,128)(2,1)S(1)} fusion(f32[1024,2048]{1,0:T(8,128)} %fusion.6, bf16[1,2048,768]{2,1,0:T(8,128)(2,1)} %param.13, bf16[128,8,768]{2,1,0:T(8,128)(2,1)} %all-to-all-done), kind=kOutput, calls=%fused_computation.2 | convolution fusion | flops 3227516928 | bytes 17301504 | tf_op jit(solution)/shard_map/dot_general | solution.py:37
  49.1 0.0 copy-start.1
  49.1 3.4 %fusion.17 = bf16[1,1024,768]{2,1,0:T(8,128)(2,1)S(1)} fusion(bf16[1024,2048]{1,0:T(8,128)(2,1)S(1)} %select_convert_fusion, bf16[1,768,2048]{2,1,0:T(8,128)(2,1)S(1)} %copy-done), kind=kOutput, calls=%fused_computation.22 | convolution fusion | flops 3222011904 | bytes 8912896 | tf_op jit(solution)/shard_map/dot_general | solution.py:44
  52.5 0.0 copy-done.1
  52.5 4.1 %copy.19 = bf16[1,1024,768]{2,0,1:T(2,128)(2,1)} copy(bf16[1,1024,768]{2,1,0:T(8,128)(2,1)S(1)} %fusion.17) | data formatting | bytes 3145728 | tf_op jit(solution)/shard_map/reshape | solution.py:48
  56.6 0.5 broadcast.34
  57.1 12.6 %reduce = bf16[1024,768]{1,0:T(8,128)(2,1)} reduce(bf16[1024,1,768]{2,1,0:T(2,128)(2,1)} %bitcast.42, bf16[]{:T(256)} %broadcast.34), dimensions={1}, to_apply=%bitcast.40.reduce_sub_computation | reduce | bytes 3145730
  69.7 4.6 %reshape.47 = bf16[128,2,3072]{2,1,0:T(2,128)(2,1)} reshape(bf16[1024,768]{1,0:T(8,128)(2,1)} %reduce) | data formatting | bytes 3145728
  74.3 5.8 %all-to-all-start.1 = ((bf16[128,2,3072]{2,1,0:T(2,128)(2,1)}), bf16[128,2,3072]{2,1,0:T(2,128)(2,1)}, u32[]{:S(2)}, u32[]{:S(2)}) async-start(bf16[128,2,3072]{2,1,0:T(2,128)(2,1)} %reshape.47), calls=%async_computation.1 | async-start | bytes 3145728 | tf_op jit(solution)/shard_map/all_to_all | solution.py:47
  80.1 8.9 %convolution_bitcast_fusion = f32[1,768,2048]{1,2,0:T(8,128)} fusion(bf16[1024,2048]{1,0:T(8,128)(2,1)} %copy-done.1, bf16[1,1024,768]{2,1,0:T(8,128)(2,1)} %param.11), kind=kOutput, calls=%fused_computation.6 | convolution fusion | flops 3221225472 | bytes 12058624 | tf_op jit(solution)/shard_map/dot_general | solution.py:41
  89.0 6.6 %copy.14 = f32[1,768,2048]{2,1,0:T(8,128)} copy(f32[1,768,2048]{1,2,0:T(8,128)} %convolution_bitcast_fusion) | data formatting | bytes 12582912
  95.6 10.0 %fusion.2 = f32[1,2048,768]{2,1,0:T(8,128)} fusion(f32[1024,2048]{1,0:T(8,128)} %fusion.6, bf16[128,8,768]{2,1,0:T(8,128)(2,1)} %all-to-all-done), kind=kOutput, calls=%fused_computation.5 | convolution fusion | flops 3225419776 | bytes 16252928 | tf_op jit(solution)/shard_map/dot_general | solution.py:34
  105.6 0.0 all-to-all-done.1
  105.6 10.4 %reshape.48 = bf16[1024,1,768]{2,1,0:T(2,128)(2,1)} reshape(bf16[128,2,3072]{2,1,0:T(2,128)(2,1)} %all-to-all-done.1) | data formatting | bytes 3145728
  116.0 3.3 %copy.18 = bf16[1,1024,768]{2,1,0:T(8,128)(2,1)} copy(bf16[1,1024,768]{2,0,1:T(2,128)(2,1)} %bitcast.43) | data formatting | bytes 3145728
  119.3 4.7 %gather_fusion = bf16[512,768]{1,0:T(8,128)(2,1)} fusion(bf16[1024,768]{1,0:T(8,128)(2,1)} %bitcast.41, s32[1024]{0:T(1024)S(1)} %pad_clamp_fusion), kind=kCustom, calls=%fused_computation | custom fusion | bytes 1574912 | tf_op jit(solution)/shard_map/jit(_take)/gather | solution.py:55
  124.0 2.2 %select_select_fusion = bf16[512,768]{1,0:T(8,128)(2,1)} fusion(bf16[512,768]{1,0:T(8,128)(2,1)} %gather_fusion, pred[512]{0:T(512)(128)(4,1)S(1)} %get-tuple-element.12, pred[512]{0:T(512)(128)(4,1)S(1)} %get-tuple-element.14), kind=kLoop, calls=%fused_computation.25 | loop fusion | flops 786432 | bytes 1573888 | tf_op jit(solution)/shard_map/jit(_where)/select_n | solution.py:56
  (2 shorter events, 0.0 us)
Async XLA Ops:
  0.6 16.4 %copy-start = (bf16[1,768,2048]{2,1,0:T(8,128)(2,1)S(1)}, bf16[1,768,2048]{2,1,0:T(8,128)(2,1)}, u32[]{:S(2)}) copy-start(bf16[1,768,2048]{2,1,0:T(8,128)(2,1)} %param.12) | copy-start | bytes 9437188
  5.0 35.8 %all-to-all-start = ((bf16[128,8,768]{2,1,0:T(8,128)(2,1)}), bf16[128,8,768]{2,1,0:T(8,128)(2,1)}, u32[]{:S(2)}, u32[]{:S(2)}) async-start(bf16[128,8,768]{2,1,0:T(8,128)(2,1)} %fusion.20), calls=%async_computation | async-start | bytes 3145728 | tf_op jit(solution)/shard_map/all_to_all | solution.py:21
  49.1 3.5 %copy-start.1 = (bf16[1024,2048]{1,0:T(8,128)(2,1)}, bf16[1024,2048]{1,0:T(8,128)(2,1)S(1)}, u32[]{:S(2)}) copy-start(bf16[1024,2048]{1,0:T(8,128)(2,1)S(1)} %select_convert_fusion) | copy-start | bytes 12582916
  74.3 31.3 %all-to-all-start.1 = ((bf16[128,2,3072]{2,1,0:T(2,128)(2,1)}), bf16[128,2,3072]{2,1,0:T(2,128)(2,1)}, u32[]{:S(2)}, u32[]{:S(2)}) async-start(bf16[128,2,3072]{2,1,0:T(2,128)(2,1)} %reshape.47), calls=%async_computation.1 | async-start | bytes 3145728 | tf_op jit(solution)/shard_map/all_to_all | solution.py:47
where the time goes:
time: 127 us; the launch traced here: 126 us
  matrix products  41.3 us (33%)
  local copies, waits for them, and re-layouts  34.1 us (27%)
  starting transfers between devices  17.7 us (14%)
  waiting for transfers between devices  16.7 us (13%)
  other arithmetic  15.7 us (12%)
    unnamed x9, local copies, waits for them, and re-layouts  25.3 us
    all_to_all x1, waiting for transfers between devices, local(): lax.all_to_all(outgoing.reshape(experts, capacity, width), ('group', 'ran...  16.7 us
    unnamed x1, other arithmetic  12.6 us
    all_to_all x1, starting transfers between devices, local(): lax.all_to_all(outgoing.reshape(experts, capacity, width), ('group', 'ran...  11.9 us
    dot_general x1, matrix products, local(): lax.dot_general(hidden, grad_rows, (((0,), (0,)), ((), ())), preferred_el...  10 us
    dot_general x1, matrix products, local(): lax.dot_general(inputs, grad_hidden, (((0,), (0,)), ((), ())), preferred_...  8.9 us
    dot_general x1, matrix products, local(): lax.dot_general(grad_rows, second, (((1,), (1,)), ((), ())), preferred_el...  8.26 us
    dot_general x1, matrix products, local(): pre = jnp.dot(inputs, first, preferred_element_type=jnp.float32)  7.1 us
  transfers between devices with their start and end apart: 2, of which 1 were waited for; matrix products, arithmetic and copies ran while one was open for 26% of the time, Pallas kernels for 0%

commit v1 on v0

v1 whole, which is shorter than its diff:
```python
import functools

import jax
import jax.numpy as jnp
from jax import lax
from jax.experimental import pallas as pl
from jax.experimental.pallas import tpu as pltpu
from jax.sharding import PartitionSpec as P

MESH = pl.DeviceIdType.MESH
BF16, F32 = jnp.bfloat16, jnp.float32
NT = (((1,), (1,)), ((), ()))
TN = (((0,), (0,)), ((), ()))
GROUPS = (((1, 0), (3, 0)), ((1, 1), (3, 1)), ((2, 0), (0, 1)), ((2, 1), (0, 0)))
CAP = 8
SIDE = 4


def dot(a, b, dims=(((1,), (0,)), ((), ()))):
    return lax.dot_general(a, b, dims, preferred_element_type=F32)


def exchange_kernel(
    gate_ref, expert_ref, slot_ref, grad_hbm, inputs_hbm, w_in_hbm, w_out_hbm,
    back_ref, pick_ref, grad_first_ref, grad_second_ref,
    grad, inputs, inputs_t, w_in, w_out, sent, arrived, row_grad, hidden, grad_hidden,
    load_sem, own_sem, send_sem, recv_sem, sync_a, sync_b,
):
    group, rank = lax.axis_index("group"), lax.axis_index("rank")
    x, y, z, core = rank // SIDE, rank % SIDE, group // 2, group % 2
    me = group * 16 + rank
    tokens, width = grad.shape
    rows = inputs.shape[0]
    hid = hidden.shape[1]
    quarter = rows // 4

    def device(dx, dy, dz, dc):
        return (lax.rem(z + dz, SIDE) * 2 + lax.rem(core + dc, 2), lax.rem(x + dx, SIDE) * SIDE + lax.rem(y + dy, SIDE))

    barrier = pltpu.get_barrier_semaphore()
    along_x = [device(i, 0, 0, c) for i in range(4) for c in range(2) if i + c > 0]
    along_y = [device(0, i, 0, 0) for i in (1, 2, 3)]
    along_z = [device(0, 0, i, 0) for i in (1, 2, 3)]
    for d in along_x + along_y + along_z:
        pl.semaphore_signal(barrier, inc=1, device_id=d, device_id_type=MESH)

    load_grad = pltpu.make_async_copy(grad_hbm, grad, load_sem.at[0])
    load_grad.start()
    load_w_in = pltpu.make_async_copy(w_in_hbm, w_in, load_sem.at[1])
    load_w_in.start()
    load_rows = []
    for j, pair in enumerate(GROUPS):
        for i, (dz, dc) in enumerate(pair):
            g = lax.rem(z + dz, SIDE) * 2 + lax.rem(core + dc, 2)
            at = (j * 2 + i) * 128
            load_rows.append(
                pltpu.make_async_copy(
                    inputs_hbm.at[pl.ds(pl.multiple_of(g * 128, 128), 128)], inputs.at[pl.ds(at, 128)], load_sem.at[2 + j * 2 + i]
                )
            )
            load_rows[-1].start()
    load_w_out = pltpu.make_async_copy(w_out_hbm, w_out, load_sem.at[10])
    load_w_out.start()

    gate = gate_ref[...]
    high = gate.astype(BF16)
    rest = gate - high.astype(F32)
    middle = rest.astype(BF16)
    low = (rest - middle.astype(F32)).astype(BF16)
    gates = [jnp.broadcast_to(part, (128, tokens)) for part in (high, middle, low)]
    target = jnp.where(slot_ref[...] >= 0, expert_ref[...] * CAP + slot_ref[...], -1)
    load_grad.wait()

    def fill(q):
        at = lax.broadcasted_iota(jnp.int32, (quarter, tokens), 0) + q * quarter
        table = (at == target).astype(BF16)
        pick_ref[pl.ds(pl.multiple_of(q * quarter, quarter), quarter), :] = table
        factor = dot(table, gates[0], NT) + dot(table, gates[1], NT) + dot(table, gates[2], NT)
        factor = jnp.concatenate([factor] * (width // 128), axis=1)
        block = dot(table, grad[...]) * factor
        sent[pl.ds(q * (quarter // CAP), quarter // CAP)] = block.reshape(quarter // CAP, CAP, width).astype(BF16)

    fill(0)
    pl.semaphore_wait(barrier, 13)
    for d in along_y:
        pl.semaphore_signal(sync_a, inc=1, device_id=d, device_id_type=MESH)
    fill(1)
    pl.semaphore_wait(sync_a, 3)
    for d in along_z:
        pl.semaphore_signal(sync_b, inc=1, device_id=d, device_id_type=MESH)
    fill(2)
    fill(3)
    pl.semaphore_wait(sync_b, 3)

    def send(j, out):
        for i, (dz, dc) in enumerate(GROUPS[j]):
            own = dz == 0 and dc == 0
            g = lax.rem(z + dz, SIDE) * 2 + lax.rem(core + dc, 2)
            there = i if dz in (0, 2) else 1 - i

            def one(k, carry):
                r = lax.rem(x + k // SIDE, SIDE) * SIDE + lax.rem(y + k % SIDE, SIDE)
                if out:
                    src, dst = sent.at[g * 16 + r], arrived.at[(j * 2 + there) * 16 + rank]
                    sems = (send_sem.at[0], recv_sem.at[j])
                else:
                    src, dst = row_grad.at[(j * 2 + i) * 16 + r], back_ref.at[me]
                    sems = (send_sem.at[1], recv_sem.at[4])
                pltpu.make_async_remote_copy(src, dst, *sems, device_id=(g, r), device_id_type=MESH).start()
                return carry

            lax.fori_loop(1 if own else 0, 16, one, 0)
            if own:
                if out:
                    pltpu.make_async_copy(sent.at[me], arrived.at[(j * 2 + i) * 16 + rank], own_sem).start()
                else:
                    pltpu.make_async_copy(row_grad.at[(j * 2 + i) * 16 + rank], back_ref.at[me], own_sem).start()

    for j in range(4):
        send(j, True)

    load_w_in.wait()
    for c in load_rows:
        c.wait()

    @pl.loop(0, 4)
    def _(p):
        at = pl.ds(pl.multiple_of(p * quarter, quarter), quarter)
        for n in range(0, hid, 512):
            pre = dot(inputs[at, :], w_in[:, n : n + 512])
            hidden[at, n : n + 512] = jnp.maximum(pre, 0.0).astype(BF16)

    inputs_t[...] = inputs[...].T
    load_w_out.wait()

    for j in range(4):
        count = 31 if (0, 0) in GROUPS[j] else 32
        got = arrived.at[pl.ds(0, count)]
        pltpu.make_async_copy(got, got, recv_sem.at[j]).wait()
        if count == 31:
            pltpu.make_async_copy(sent.at[me], arrived.at[j * 32 + rank], own_sem).wait()
        block = arrived[pl.ds(j * 32, 32)].reshape(quarter, width)
        at = pl.ds(j * quarter, quarter)
        for n in range(0, hid, 512):
            up = dot(block, w_out[n : n + 512, :], NT)
            grad_hidden[at, n : n + 512] = jnp.where(hidden[at, n : n + 512].astype(F32) > 0, up, 0.0).astype(BF16)
        down = dot(grad_hidden[at, :], w_in[...], NT)
        row_grad[pl.ds(j * 32, 32)] = down.reshape(32, CAP, width).astype(BF16)
        send(j, False)

    @pl.loop(0, hid, step=256)
    def _(n):
        at = pl.ds(pl.multiple_of(n, 256), 256)
        grad_second_ref[at, :] = dot(hidden[:, at], arrived[...].reshape(rows, width), TN)

    @pl.loop(0, hid, step=256)
    def _(n):
        at = pl.ds(pl.multiple_of(n, 256), 256)
        grad_first_ref[:, at] = dot(inputs_t[...], grad_hidden[:, at])

    pltpu.make_async_copy(row_grad.at[0], back_ref.at[me], own_sem).wait()
    most = sent.at[pl.ds(0, 127)]
    pltpu.make_async_copy(most, most, send_sem.at[0]).wait()
    most = row_grad.at[pl.ds(0, 127)]
    pltpu.make_async_copy(most, most, send_sem.at[1]).wait()
    most = back_ref.at[pl.ds(0, 127)]
    pltpu.make_async_copy(most, most, recv_sem.at[4]).wait()


def finish_kernel(back_ref, pick_ref, first_ref, second_ref, grad_in_hbm, first_hbm, second_hbm, grad_in, sems):
    copies = [
        pltpu.make_async_copy(first_ref, first_hbm, sems.at[0]),
        pltpu.make_async_copy(second_ref, second_hbm, sems.at[1]),
    ]
    for c in copies:
        c.start()
    rows, tokens = pick_ref.shape
    grad_in[...] = dot(pick_ref[...], back_ref[...].reshape(rows, grad_in.shape[1]), TN).astype(BF16)
    copies.append(pltpu.make_async_copy(grad_in, grad_in_hbm, sems.at[2]))
    copies[-1].start()
    for c in copies:
        c.wait()


def local(grad_out, gate_prob, expert_index, slot, saved_inputs, w_in, w_out):
    tokens, width = grad_out.shape
    rows, hid = saved_inputs.shape[1], w_in.shape[2]
    experts = rows // CAP
    vmem, hbm = pl.BlockSpec(memory_space=pltpu.VMEM), pl.BlockSpec(memory_space=pl.ANY)
    back, pick, first, second = pl.pallas_call(
        exchange_kernel,
        out_shape=(
            pltpu.VMEM((experts, CAP, width), BF16),
            pltpu.VMEM((rows, tokens), BF16),
            pltpu.VMEM((width, hid), F32),
            pltpu.VMEM((hid, width), F32),
        ),
        in_specs=[vmem] * 3 + [hbm] * 4,
        out_specs=(vmem,) * 4,
        scratch_shapes=[
            pltpu.VMEM((tokens, width), BF16),
            pltpu.VMEM((rows, width), BF16),
            pltpu.VMEM((width, rows), BF16),
            pltpu.VMEM((width, hid), BF16),
            pltpu.VMEM((hid, width), BF16),
            pltpu.VMEM((experts, CAP, width), BF16),
            pltpu.VMEM((experts, CAP, width), BF16),
            pltpu.VMEM((experts, CAP, width), BF16),
            pltpu.VMEM((rows, hid), BF16),
            pltpu.VMEM((rows, hid), BF16),
            pltpu.SemaphoreType.DMA((11,)),
            pltpu.SemaphoreType.DMA,
            pltpu.SemaphoreType.DMA((2,)),
            pltpu.SemaphoreType.DMA((5,)),
            pltpu.SemaphoreType.REGULAR,
            pltpu.SemaphoreType.REGULAR,
        ],
        name="exchange",
        compiler_params=pltpu.CompilerParams(collective_id=0, has_side_effects=True, vmem_limit_bytes=40 << 20),
    )(
        gate_prob.reshape(1, tokens),
        expert_index.reshape(1, tokens),
        slot.reshape(1, tokens),
        grad_out,
        saved_inputs[0],
        w_in[0],
        w_out[0],
    )
    grad_in, grad_first, grad_second = pl.pallas_call(
        finish_kernel,
        out_shape=(
            jax.ShapeDtypeStruct((tokens, width), BF16),
            jax.ShapeDtypeStruct((width, hid), F32),
            jax.ShapeDtypeStruct((hid, width), F32),
        ),
        in_specs=[vmem] * 4,
        out_specs=(hbm,) * 3,
        scratch_shapes=[pltpu.VMEM((tokens, width), BF16), pltpu.SemaphoreType.DMA((3,))],
        name="finish",
        compiler_params=pltpu.CompilerParams(vmem_limit_bytes=24 << 20),
    )(*(pltpu.with_memory_space_constraint(a, pltpu.VMEM) for a in (back, pick, first, second)))
    return grad_in, grad_first[None], grad_second[None]


def solution(mesh):
    spec1, spec2, spec3 = (P(("group", "rank"), *(None,) * n) for n in range(3))
    return jax.shard_map(
        local,
        mesh=mesh,
        in_specs=(spec2, spec1, spec1, spec1, spec3, spec3, spec3),
        out_specs=(spec2, spec3, spec3),
        check_vma=False,
    )
```

time: 127 us -> 68.9 us (0.54)
  the two profiles are of different devices: /device:TPU:1 before, /device:TPU:2 now
where the time goes in v1:
time: 68.9 us; the launch traced here: 68.7 us
  Pallas kernels  68.1 us (99%)
    pallas_call x1, Pallas kernels, local(): pl.pallas_call(exchange_kernel, out_shape=(pltpu.VMEM((experts, CAP, widt...  63.2 us
    pallas_call x1, Pallas kernels, local(): pl.pallas_call(finish_kernel, out_shape=(jax.ShapeDtypeStruct((tokens, wi...  4.87 us

profile of v1, /device:TPU:2, one launch (start us, length us, event | category | flops | bytes accessed | tf_op | source)
XLA Modules:
  0.0 68.7 jit_solution(8904559065145710939)
XLA Ops:
  0.6 63.2 %exchange.1 = (bf16[128,8,768]{2,1,0:T(8,128)(2,1)S(1)}, bf16[1024,512]{1,0:T(8,128)(2,1)S(1)}, f32[768,2048]{1,0:T(8,128)S(1)}, f32[2048,768]{1,0:T(8,128)S(1)}) custom-call(f32[1,512]{1,0:T(1,128)} %bitcast.11, s32[1,512]{1,0:T(1,128)} %bitcast.12, s32[1,512]{1,0:T(1,128)} %bitcast.13, bf16[512,768]{1,0:T(8,128)(2,1)} %grad_hbm.1, ...), custom_call_target="tpu_custom_call" | custom-call | tf_op jit(solution)/shard_map/exchange/pallas_call | solution.py:190
  63.8 4.9 %finish.1 = (bf16[512,768]{1,0:T(8,128)(2,1)}, f32[768,2048]{1,0:T(8,128)}, f32[2048,768]{1,0:T(8,128)}) custom-call(bf16[128,8,768]{2,1,0:T(8,128)(2,1)S(1)} %get-tuple-element.10.back_ref, bf16[1024,512]{1,0:T(8,128)(2,1)S(1)} %get-tuple-element.11.pick_ref, f32[768,2048]{1,0:T(8,128)S(1)} %get-tuple-element.12.first_ref, ...), custom_call_target="tpu_custom_call" | custom-call | tf_op jit(solution)/shard_map/finish/pallas_call | solution.py:229

commit v2 on v1

--- a/solution.py
+++ b/solution.py
@@ -14,6 +14,7 @@
 GROUPS = (((1, 0), (3, 0)), ((1, 1), (3, 1)), ((2, 0), (0, 1)), ((2, 1), (0, 0)))
 CAP = 8
 SIDE = 4
+PIECES = 1
 
 
 def dot(a, b, dims=(((1,), (0,)), ((), ()))):
@@ -69,54 +70,62 @@
     low = (rest - middle.astype(F32)).astype(BF16)
     gates = [jnp.broadcast_to(part, (128, tokens)) for part in (high, middle, low)]
     target = jnp.where(slot_ref[...] >= 0, expert_ref[...] * CAP + slot_ref[...], -1)
+    pl.semaphore_wait(barrier, 13)
+    for d in along_y:
+        pl.semaphore_signal(sync_a, inc=1, device_id=d, device_id_type=MESH)
+    pl.semaphore_wait(sync_a, 3)
+    for d in along_z:
+        pl.semaphore_signal(sync_b, inc=1, device_id=d, device_id_type=MESH)
     load_grad.wait()
 
-    def fill(q):
-        at = lax.broadcasted_iota(jnp.int32, (quarter, tokens), 0) + q * quarter
+    def group_at(j, i):
+        dz, dc = GROUPS[j][i]
+        return lax.rem(z + dz, SIDE) * 2 + lax.rem(core + dc, 2)
+
+    def fill(g):
+        at = lax.broadcasted_iota(jnp.int32, (128, tokens), 0) + g * 128
         table = (at == target).astype(BF16)
-        pick_ref[pl.ds(pl.multiple_of(q * quarter, quarter), quarter), :] = table
+        pick_ref[pl.ds(pl.multiple_of(g * 128, 128), 128), :] = table
         factor = dot(table, gates[0], NT) + dot(table, gates[1], NT) + dot(table, gates[2], NT)
         factor = jnp.concatenate([factor] * (width // 128), axis=1)
         block = dot(table, grad[...]) * factor
-        sent[pl.ds(q * (quarter // CAP), quarter // CAP)] = block.reshape(quarter // CAP, CAP, width).astype(BF16)
-
-    fill(0)
-    pl.semaphore_wait(barrier, 13)
-    for d in along_y:
-        pl.semaphore_signal(sync_a, inc=1, device_id=d, device_id_type=MESH)
-    fill(1)
-    pl.semaphore_wait(sync_a, 3)
-    for d in along_z:
-        pl.semaphore_signal(sync_b, inc=1, device_id=d, device_id_type=MESH)
-    fill(2)
-    fill(3)
-    pl.semaphore_wait(sync_b, 3)
+        sent[pl.ds(g * 16, 16)] = block.reshape(16, CAP, width).astype(BF16)
 
     def send(j, out):
-        for i, (dz, dc) in enumerate(GROUPS[j]):
-            own = dz == 0 and dc == 0
-            g = lax.rem(z + dz, SIDE) * 2 + lax.rem(core + dc, 2)
-            there = i if dz in (0, 2) else 1 - i
-
-            def one(k, carry):
-                r = lax.rem(x + k // SIDE, SIDE) * SIDE + lax.rem(y + k % SIDE, SIDE)
-                if out:
-                    src, dst = sent.at[g * 16 + r], arrived.at[(j * 2 + there) * 16 + rank]
-                    sems = (send_sem.at[0], recv_sem.at[j])
-                else:
-                    src, dst = row_grad.at[(j * 2 + i) * 16 + r], back_ref.at[me]
-                    sems = (send_sem.at[1], recv_sem.at[4])
-                pltpu.make_async_remote_copy(src, dst, *sems, device_id=(g, r), device_id_type=MESH).start()
-                return carry
-
-            lax.fori_loop(1 if own else 0, 16, one, 0)
-            if own:
-                if out:
-                    pltpu.make_async_copy(sent.at[me], arrived.at[(j * 2 + i) * 16 + rank], own_sem).start()
-                else:
-                    pltpu.make_async_copy(row_grad.at[(j * 2 + i) * 16 + rank], back_ref.at[me], own_sem).start()
+        def copy_of(i, dx, dy):
+            g = group_at(j, i)
+            there = i if GROUPS[j][i][0] in (0, 2) else 1 - i
+            r = lax.rem(x + dx, SIDE) * SIDE + lax.rem(y + dy, SIDE)
+            if out:
+                src, dst, end = sent.at[g * 16 + r], arrived.at[(j * 2 + there) * 16 + rank], (send_sem.at[0], recv_sem.at[j])
+            else:
+                src, dst, end = row_grad.at[(j * 2 + i) * 16 + r], back_ref.at[me], (send_sem.at[1], recv_sem.at[4])
+            return src, dst, end, (g, r)
+
+        def start(i, dx, dy):
+            src, dst, end, d = copy_of(i, dx, dy)
+            pltpu.make_async_remote_copy(src, dst, *end, device_id=d, device_id_type=MESH).start()
+
+        def swing(q):
+            return q + q // 2 - 2 * (q // 3)
+
+        def one(k, carry):
+            for i in range(2):
+                start(i, swing(k % 4), swing((k + k // 4) % 4))
+            return carry
+
+        own = (0, 0) in GROUPS[j]
+        if own:
+            start(0, 0, 0)
+            src, dst, _, _ = copy_of(1, 0, 0)
+            pltpu.make_async_copy(src, dst, own_sem).start()
+        lax.fori_loop(1 if own else 0, 16, one, 0)
 
     for j in range(4):
+        fill(group_at(j, 0))
+        fill(group_at(j, 1))
+        if j == 0:
+            pl.semaphore_wait(sync_b, 3)
         send(j, True)
 
     load_w_in.wait()
@@ -168,15 +177,16 @@
 
 
 def finish_kernel(back_ref, pick_ref, first_ref, second_ref, grad_in_hbm, first_hbm, second_hbm, grad_in, sems):
-    copies = [
-        pltpu.make_async_copy(first_ref, first_hbm, sems.at[0]),
-        pltpu.make_async_copy(second_ref, second_hbm, sems.at[1]),
-    ]
-    for c in copies:
-        c.start()
+    copies = []
+    for ref, to, base in ((first_ref, first_hbm, 0), (second_ref, second_hbm, PIECES)):
+        step = ref.shape[0] // PIECES
+        for p in range(PIECES):
+            at = pl.ds(p * step, step)
+            copies.append(pltpu.make_async_copy(ref.at[at], to.at[at], sems.at[base + p]))
+            copies[-1].start()
     rows, tokens = pick_ref.shape
     grad_in[...] = dot(pick_ref[...], back_ref[...].reshape(rows, grad_in.shape[1]), TN).astype(BF16)
-    copies.append(pltpu.make_async_copy(grad_in, grad_in_hbm, sems.at[2]))
+    copies.append(pltpu.make_async_copy(grad_in, grad_in_hbm, sems.at[2 * PIECES]))
     copies[-1].start()
     for c in copies:
         c.wait()
@@ -235,7 +245,7 @@
         ),
         in_specs=[vmem] * 4,
         out_specs=(hbm,) * 3,
-        scratch_shapes=[pltpu.VMEM((tokens, width), BF16), pltpu.SemaphoreType.DMA((3,))],
+        scratch_shapes=[pltpu.VMEM((tokens, width), BF16), pltpu.SemaphoreType.DMA((2 * PIECES + 1,))],
         name="finish",
         compiler_params=pltpu.CompilerParams(vmem_limit_bytes=24 << 20),
     )(*(pltpu.with_memory_space_constraint(a, pltpu.VMEM) for a in (back, pick, first, second)))

time: 68.9 us -> 54.5 us (0.79)
  the two profiles are of different devices: /device:TPU:2 before, /device:TPU:1 now
where the time goes in v2:
time: 54.5 us; the launch traced here: 54.3 us
  Pallas kernels  53.7 us (99%)
  between operations  0.64 us (1%)
    pallas_call x1, Pallas kernels, local(): pl.pallas_call(exchange_kernel, out_shape=(pltpu.VMEM((experts, CAP, widt...  48.8 us
    pallas_call x1, Pallas kernels, local(): pl.pallas_call(finish_kernel, out_shape=(jax.ShapeDtypeStruct((tokens, wi...  4.87 us

profile of v2, /device:TPU:1, one launch (start us, length us, event | category | flops | bytes accessed | tf_op | source)
XLA Modules:
  0.0 54.3 jit_solution(851363582460274956)
XLA Ops:
  0.6 48.8 %exchange.1 = (bf16[128,8,768]{2,1,0:T(8,128)(2,1)S(1)}, bf16[1024,512]{1,0:T(8,128)(2,1)S(1)}, f32[768,2048]{1,0:T(8,128)S(1)}, f32[2048,768]{1,0:T(8,128)S(1)}) custom-call(f32[1,512]{1,0:T(1,128)} %bitcast.11, s32[1,512]{1,0:T(1,128)} %bitcast.12, s32[1,512]{1,0:T(1,128)} %bitcast.13, bf16[512,768]{1,0:T(8,128)(2,1)} %grad_hbm.1, ...), custom_call_target="tpu_custom_call" | custom-call | tf_op jit(solution)/shard_map/exchange/pallas_call | solution.py:200
  49.4 4.9 %finish.1 = (bf16[512,768]{1,0:T(8,128)(2,1)}, f32[768,2048]{1,0:T(8,128)}, f32[2048,768]{1,0:T(8,128)}) custom-call(bf16[128,8,768]{2,1,0:T(8,128)(2,1)S(1)} %get-tuple-element.10.back_ref, bf16[1024,512]{1,0:T(8,128)(2,1)S(1)} %get-tuple-element.11.pick_ref, f32[768,2048]{1,0:T(8,128)S(1)} %get-tuple-element.12.first_ref, ...), custom_call_target="tpu_custom_call" | custom-call | tf_op jit(solution)/shard_map/finish/pallas_call | solution.py:239

commit v3 on v2

--- a/solution.py
+++ b/solution.py
@@ -11,7 +11,7 @@
 BF16, F32 = jnp.bfloat16, jnp.float32
 NT = (((1,), (1,)), ((), ()))
 TN = (((0,), (0,)), ((), ()))
-GROUPS = (((1, 0), (3, 0)), ((1, 1), (3, 1)), ((2, 0), (0, 1)), ((2, 1), (0, 0)))
+GROUPS = (((1, 0), (3, 0)), ((2, 0), (0, 1)), ((1, 1), (3, 1)), ((2, 1), (0, 0)))
 CAP = 8
 SIDE = 4
 PIECES = 1
@@ -22,9 +22,9 @@
 
 
 def exchange_kernel(
-    gate_ref, expert_ref, slot_ref, grad_hbm, inputs_hbm, w_in_hbm, w_out_hbm,
+    gate_hbm, expert_hbm, slot_hbm, grad_hbm, inputs_hbm, w_in_hbm, w_out_hbm,
     back_ref, pick_ref, grad_first_ref, grad_second_ref,
-    grad, inputs, inputs_t, w_in, w_out, sent, arrived, row_grad, hidden, grad_hidden,
+    gate_ref, expert_ref, slot_ref, grad, inputs, inputs_t, w_in, w_out, sent, arrived, row_grad, hidden, grad_hidden,
     load_sem, own_sem, send_sem, recv_sem, sync_a, sync_b,
 ):
     group, rank = lax.axis_index("group"), lax.axis_index("rank")
@@ -39,12 +39,16 @@
         return (lax.rem(z + dz, SIDE) * 2 + lax.rem(core + dc, 2), lax.rem(x + dx, SIDE) * SIDE + lax.rem(y + dy, SIDE))
 
     barrier = pltpu.get_barrier_semaphore()
-    along_x = [device(i, 0, 0, c) for i in range(4) for c in range(2) if i + c > 0]
-    along_y = [device(0, i, 0, 0) for i in (1, 2, 3)]
-    along_z = [device(0, 0, i, 0) for i in (1, 2, 3)]
-    for d in along_x + along_y + along_z:
+    others = [device(i, k, l, c) for l in (1, 3, 2, 0) for k in range(4) for i in range(4) for c in range(2) if i + k + l + c > 0]
+    for d in others:
         pl.semaphore_signal(barrier, inc=1, device_id=d, device_id_type=MESH)
 
+    load_tokens = [
+        pltpu.make_async_copy(src, dst, load_sem.at[11 + i])
+        for i, (src, dst) in enumerate(((gate_hbm, gate_ref), (expert_hbm, expert_ref), (slot_hbm, slot_ref)))
+    ]
+    for c in load_tokens:
+        c.start()
     load_grad = pltpu.make_async_copy(grad_hbm, grad, load_sem.at[0])
     load_grad.start()
     load_w_in = pltpu.make_async_copy(w_in_hbm, w_in, load_sem.at[1])
@@ -63,6 +67,8 @@
     load_w_out = pltpu.make_async_copy(w_out_hbm, w_out, load_sem.at[10])
     load_w_out.start()
 
+    for c in load_tokens:
+        c.wait()
     gate = gate_ref[...]
     high = gate.astype(BF16)
     rest = gate - high.astype(F32)
@@ -70,12 +76,6 @@
     low = (rest - middle.astype(F32)).astype(BF16)
     gates = [jnp.broadcast_to(part, (128, tokens)) for part in (high, middle, low)]
     target = jnp.where(slot_ref[...] >= 0, expert_ref[...] * CAP + slot_ref[...], -1)
-    pl.semaphore_wait(barrier, 13)
-    for d in along_y:
-        pl.semaphore_signal(sync_a, inc=1, device_id=d, device_id_type=MESH)
-    pl.semaphore_wait(sync_a, 3)
-    for d in along_z:
-        pl.semaphore_signal(sync_b, inc=1, device_id=d, device_id_type=MESH)
     load_grad.wait()
 
     def group_at(j, i):
@@ -125,7 +125,7 @@
         fill(group_at(j, 0))
         fill(group_at(j, 1))
         if j == 0:
-            pl.semaphore_wait(sync_b, 3)
+            pl.semaphore_wait(barrier, 127)
         send(j, True)
 
     load_w_in.wait()
@@ -205,9 +205,12 @@
             pltpu.VMEM((width, hid), F32),
             pltpu.VMEM((hid, width), F32),
         ),
-        in_specs=[vmem] * 3 + [hbm] * 4,
+        in_specs=[hbm] * 7,
         out_specs=(vmem,) * 4,
         scratch_shapes=[
+            pltpu.VMEM((1, tokens), F32),
+            pltpu.VMEM((1, tokens), jnp.int32),
+            pltpu.VMEM((1, tokens), jnp.int32),
             pltpu.VMEM((tokens, width), BF16),
             pltpu.VMEM((rows, width), BF16),
             pltpu.VMEM((width, rows), BF16),
@@ -218,7 +221,7 @@
             pltpu.VMEM((experts, CAP, width), BF16),
             pltpu.VMEM((rows, hid), BF16),
             pltpu.VMEM((rows, hid), BF16),
-            pltpu.SemaphoreType.DMA((11,)),
+            pltpu.SemaphoreType.DMA((14,)),
             pltpu.SemaphoreType.DMA,
             pltpu.SemaphoreType.DMA((2,)),
             pltpu.SemaphoreType.DMA((5,)),

time: 54.5 us -> 53.1 us (0.974)
  Pallas kernels: 53.7 us -> 52.4 us
    pallas_call x1, Pallas kernels: 48.8 us -> 47.5 us  [local(): pl.pallas_call(exchange_kernel, out_shape=(pltpu.VMEM((experts, CAP, widt...]
where the time goes in v3:
time: 53.1 us; the launch traced here: 53 us
  Pallas kernels  52.4 us (99%)
  between operations  0.64 us (1%)
    pallas_call x1, Pallas kernels, local(): pl.pallas_call(exchange_kernel, out_shape=(pltpu.VMEM((experts, CAP, widt...  47.5 us
    pallas_call x1, Pallas kernels, local(): pl.pallas_call(finish_kernel, out_shape=(jax.ShapeDtypeStruct((tokens, wi...  4.87 us

profile of v3, /device:TPU:1, one launch (start us, length us, event | category | flops | bytes accessed | tf_op | source)
XLA Modules:
  0.0 53.0 jit_solution(4733774696437309795)
XLA Ops:
  0.6 47.5 %exchange.1 = (bf16[128,8,768]{2,1,0:T(8,128)(2,1)S(1)}, bf16[1024,512]{1,0:T(8,128)(2,1)S(1)}, f32[768,2048]{1,0:T(8,128)S(1)}, f32[2048,768]{1,0:T(8,128)S(1)}) custom-call(f32[1,512]{1,0:T(1,128)} %bitcast.11, s32[1,512]{1,0:T(1,128)} %bitcast.12, s32[1,512]{1,0:T(1,128)} %bitcast.13, bf16[512,768]{1,0:T(8,128)(2,1)} %grad_hbm.1, ...), custom_call_target="tpu_custom_call" | custom-call | tf_op jit(solution)/shard_map/exchange/pallas_call | solution.py:200
  48.2 4.9 %finish.1 = (bf16[512,768]{1,0:T(8,128)(2,1)}, f32[768,2048]{1,0:T(8,128)}, f32[2048,768]{1,0:T(8,128)}) custom-call(bf16[128,8,768]{2,1,0:T(8,128)(2,1)S(1)} %get-tuple-element.10.back_ref, bf16[1024,512]{1,0:T(8,128)(2,1)S(1)} %get-tuple-element.11.pick_ref, f32[768,2048]{1,0:T(8,128)S(1)} %get-tuple-element.12.first_ref, ...), custom_call_target="tpu_custom_call" | custom-call | tf_op jit(solution)/shard_map/finish/pallas_call | solution.py:242

commit v4 on v3

--- a/solution.py
+++ b/solution.py
@@ -11,7 +11,7 @@
 BF16, F32 = jnp.bfloat16, jnp.float32
 NT = (((1,), (1,)), ((), ()))
 TN = (((0,), (0,)), ((), ()))
-GROUPS = (((1, 0), (3, 0)), ((2, 0), (0, 1)), ((1, 1), (3, 1)), ((2, 1), (0, 0)))
+GROUPS = (((1, 1), (3, 1)), ((2, 1), (0, 0)), ((1, 0), (3, 0)), ((2, 0), (0, 1)))
 CAP = 8
 SIDE = 4
 PIECES = 1

time: 53.1 us -> 52.8 us (level)
  no operation moved by 1% of the time
where the time goes in v4:
time: 52.8 us; the launch traced here: 52.7 us
  Pallas kernels  52 us (98%)
  between operations  0.64 us (1%)
    pallas_call x1, Pallas kernels, local(): pl.pallas_call(exchange_kernel, out_shape=(pltpu.VMEM((experts, CAP, widt...  47.2 us
    pallas_call x1, Pallas kernels, local(): pl.pallas_call(finish_kernel, out_shape=(jax.ShapeDtypeStruct((tokens, wi...  4.87 us

profile of v4, /device:TPU:1, one launch (start us, length us, event | category | flops | bytes accessed | tf_op | source)
XLA Modules:
  0.0 52.7 jit_solution(14709659613636693588)
XLA Ops:
  0.6 47.2 %exchange.1 = (bf16[128,8,768]{2,1,0:T(8,128)(2,1)S(1)}, bf16[1024,512]{1,0:T(8,128)(2,1)S(1)}, f32[768,2048]{1,0:T(8,128)S(1)}, f32[2048,768]{1,0:T(8,128)S(1)}) custom-call(f32[1,512]{1,0:T(1,128)} %bitcast.11, s32[1,512]{1,0:T(1,128)} %bitcast.12, s32[1,512]{1,0:T(1,128)} %bitcast.13, bf16[512,768]{1,0:T(8,128)(2,1)} %grad_hbm.1, ...), custom_call_target="tpu_custom_call" | custom-call | tf_op jit(solution)/shard_map/exchange/pallas_call | solution.py:200
  47.8 4.9 %finish.1 = (bf16[512,768]{1,0:T(8,128)(2,1)}, f32[768,2048]{1,0:T(8,128)}, f32[2048,768]{1,0:T(8,128)}) custom-call(bf16[128,8,768]{2,1,0:T(8,128)(2,1)S(1)} %get-tuple-element.10.back_ref, bf16[1024,512]{1,0:T(8,128)(2,1)S(1)} %get-tuple-element.11.pick_ref, f32[768,2048]{1,0:T(8,128)S(1)} %get-tuple-element.12.first_ref, ...), custom_call_target="tpu_custom_call" | custom-call | tf_op jit(solution)/shard_map/finish/pallas_call | solution.py:242

commit v5 on v4

--- a/solution.py
+++ b/solution.py
@@ -111,7 +111,7 @@
 
         def one(k, carry):
             for i in range(2):
-                start(i, swing(k % 4), swing((k + k // 4) % 4))
+                start(i, swing((k + k // 4) % 4), swing(k % 4))
             return carry
 
         own = (0, 0) in GROUPS[j]
@@ -138,6 +138,7 @@
         for n in range(0, hid, 512):
             pre = dot(inputs[at, :], w_in[:, n : n + 512])
             hidden[at, n : n + 512] = jnp.maximum(pre, 0.0).astype(BF16)
+            grad_hidden[at, n : n + 512] = (pre > 0).astype(BF16)
 
     inputs_t[...] = inputs[...].T
     load_w_out.wait()
@@ -152,7 +153,7 @@
         at = pl.ds(j * quarter, quarter)
         for n in range(0, hid, 512):
             up = dot(block, w_out[n : n + 512, :], NT)
-            grad_hidden[at, n : n + 512] = jnp.where(hidden[at, n : n + 512].astype(F32) > 0, up, 0.0).astype(BF16)
+            grad_hidden[at, n : n + 512] = jnp.where(grad_hidden[at, n : n + 512].astype(F32) > 0, up, 0.0).astype(BF16)
         down = dot(grad_hidden[at, :], w_in[...], NT)
         row_grad[pl.ds(j * 32, 32)] = down.reshape(32, CAP, width).astype(BF16)
         send(j, False)

time: 52.8 us -> 52.8 us (level)
  no operation moved by 1% of the time
where the time goes in v5:
time: 52.8 us; the launch traced here: 52.7 us
  Pallas kernels  52.1 us (99%)
  between operations  0.64 us (1%)
    pallas_call x1, Pallas kernels, local(): pl.pallas_call(exchange_kernel, out_shape=(pltpu.VMEM((experts, CAP, widt...  47.2 us
    pallas_call x1, Pallas kernels, local(): pl.pallas_call(finish_kernel, out_shape=(jax.ShapeDtypeStruct((tokens, wi...  4.87 us

profile of v5, /device:TPU:1, one launch (start us, length us, event | category | flops | bytes accessed | tf_op | source)
XLA Modules:
  0.0 52.7 jit_solution(7342518713959933508)
XLA Ops:
  0.6 47.2 %exchange.1 = (bf16[128,8,768]{2,1,0:T(8,128)(2,1)S(1)}, bf16[1024,512]{1,0:T(8,128)(2,1)S(1)}, f32[768,2048]{1,0:T(8,128)S(1)}, f32[2048,768]{1,0:T(8,128)S(1)}) custom-call(f32[1,512]{1,0:T(1,128)} %bitcast.11, s32[1,512]{1,0:T(1,128)} %bitcast.12, s32[1,512]{1,0:T(1,128)} %bitcast.13, bf16[512,768]{1,0:T(8,128)(2,1)} %grad_hbm.1, ...), custom_call_target="tpu_custom_call" | custom-call | tf_op jit(solution)/shard_map/exchange/pallas_call | solution.py:201
  47.9 4.9 %finish.1 = (bf16[512,768]{1,0:T(8,128)(2,1)}, f32[768,2048]{1,0:T(8,128)}, f32[2048,768]{1,0:T(8,128)}) custom-call(bf16[128,8,768]{2,1,0:T(8,128)(2,1)S(1)} %get-tuple-element.10.back_ref, bf16[1024,512]{1,0:T(8,128)(2,1)S(1)} %get-tuple-element.11.pick_ref, f32[768,2048]{1,0:T(8,128)S(1)} %get-tuple-element.12.first_ref, ...), custom_call_target="tpu_custom_call" | custom-call | tf_op jit(solution)/shard_map/finish/pallas_call | solution.py:243
